TPU v7x, 32 devices: a whole 2x2x4 slice. The times are simulated.
32 devices in a mesh: dp: 8 (over z, core), seq: 4 (over y, x).
Axes of the slice: x: 2, y: 2, z: 4, core: 2. Of those that a mesh axis runs over, the one named last changes fastest.
Arguments:
- queries: bfloat16 [8, 1024, 1024], P('dp', 'seq'), may hold values from -80 to 80
- keys: bfloat16 [8, 1024, 1024], P('dp', 'seq'), may hold values from -80 to 80
- values: bfloat16 [8, 1024, 1024], P('dp', 'seq'), may hold values from -12 to 12
- upstream: bfloat16 [8, 1024, 1024], P('dp', 'seq'), may hold values from -6 to 6
- w_out: bfloat16 [1024, 1024], replicated, may hold values from -0.1875 to 0.1875
- key_blocks: int32 [8, 8, 4], P('dp'), may hold values from 0 to 7, as said below
- block_counts: int32 [8, 8], P('dp'), may hold values from 1 to 4, as said below
Outputs:
- mixed: bfloat16 [8, 1024, 1024], P('dp', 'seq')
- grad_q: bfloat16 [8, 1024, 1024], P('dp', 'seq')
- grad_k: bfloat16 [8, 1024, 1024], P('dp', 'seq')
- grad_v: bfloat16 [8, 1024, 1024], P('dp', 'seq')
- grad_wo: float32 [1024, 1024], P('seq', 'dp')
Inputs may be any that keep to these rules, and one draw needn't show every extreme that they name: `key_blocks`: row b of a sequence's lists holds 4 distinct block numbers, the first of them b itself; entries past block_counts are valid numbers and are not used. `block_counts`: every sequence has a query block with exactly 4 used entries.
All inputs are finite; a program needn't handle non-finite values.
Results may differ from a plain program's by a relative error of at most 0.039.
Values may be sent and summed in bfloat16 or wider, within the bound.
A program may use at most 128 MiB of HBM per device.

v0:
```python
import functools
import math

import jax
import jax.numpy as jnp
from jax import lax
from jax.experimental import pallas as pl
from jax.experimental.pallas import tpu as pltpu
from jax.sharding import PartitionSpec as P

HEADS = 16


blocks_per_step = 4


def product(form, left, right):
    return jnp.einsum(form, left, right, preferred_element_type=jnp.float32)


def inner_rows(left, right):
    return lax.dot_general(
        left, right, (((0,), (0,)), ((), ())), preferred_element_type=jnp.float32
    )


def block_attention(head_q, head_k, head_v, head_g, key_lists, key_counts):
    node_count, head_count, head_width = head_q.shape
    block_count, listed = key_lists.shape
    block_rows = node_count // block_count
    steps_count = block_count // blocks_per_step
    score_scale = 1.0 / math.sqrt(head_width)
    query_groups = head_q.reshape(steps_count, blocks_per_step, block_rows, head_count, head_width)
    grad_groups = head_g.reshape(steps_count, blocks_per_step, block_rows, head_count, head_width)
    key_table = head_k.reshape(block_count, block_rows, head_count, head_width)
    value_table = head_v.reshape(block_count, block_rows, head_count, head_width)
    list_groups = key_lists.reshape(steps_count, blocks_per_step, listed)
    count_groups = key_counts.reshape(steps_count, blocks_per_step)
    slot_index = jnp.arange(listed, dtype=jnp.int32)

    def one_step(accumulated, inputs):
        key_acc, value_acc = accumulated
        query_part, grad_part, list_part, count_part = inputs
        keys_near = key_table[list_part]
        values_near = value_table[list_part]
        scores = product("gqnd,gjknd->gnqjk", query_part, keys_near) * score_scale
        usable = (slot_index[None, :] < count_part[:, None])[:, None, None, :, None]
        scores = jnp.where(usable, scores, -jnp.inf)
        highest = jnp.max(scores, axis=(3, 4), keepdims=True)
        raised = jnp.exp(scores - highest)
        probability = raised / jnp.sum(raised, axis=(3, 4), keepdims=True)
        weights = probability.astype(jnp.bfloat16)
        attended = product("gnqjk,gjknd->gqnd", weights, values_near).astype(jnp.bfloat16)
        row_delta = jnp.sum(grad_part.astype(jnp.float32) * attended.astype(jnp.float32), axis=3)
        grad_scores = product("gqnd,gjknd->gnqjk", grad_part, values_near)
        shifted = grad_scores - jnp.transpose(row_delta, (0, 2, 1))[:, :, :, None, None]
        grad_logits = (probability * shifted).astype(jnp.bfloat16)
        grad_query = (product("gnqjk,gjknd->gqnd", grad_logits, keys_near) * score_scale).astype(
            jnp.bfloat16
        )
        key_terms = product("gnqjk,gqnd->gjknd", grad_logits, query_part) * score_scale
        value_terms = product("gnqjk,gqnd->gjknd", weights, grad_part)
        flat_list = list_part.reshape(-1)
        key_acc = key_acc.at[flat_list].add(
            key_terms.reshape(-1, block_rows, head_count, head_width)
        )
        value_acc = value_acc.at[flat_list].add(
            value_terms.reshape(-1, block_rows, head_count, head_width)
        )
        return ((key_acc, value_acc), (attended, grad_query))

    empty = jnp.zeros((block_count, block_rows, head_count, head_width), jnp.float32)
    (key_acc, value_acc), (attended, grad_query) = lax.scan(
        one_step, (empty, empty), (query_groups, grad_groups, list_groups, count_groups)
    )
    shape = (node_count, head_count, head_width)
    return (
        attended.reshape(shape),
        grad_query.reshape(shape),
        key_acc.astype(jnp.bfloat16).reshape(shape),
        value_acc.astype(jnp.bfloat16).reshape(shape),
    )


def project_back(up_rows, w_out):
    return lax.dot_general(
        up_rows, w_out, (((1,), (1,)), ((), ())), preferred_element_type=jnp.float32
    ).astype(jnp.bfloat16)


def local_plain(queries, keys, values, upstream, w_out, key_blocks, block_counts):
    local_rows = queries.shape[1]
    width = queries.shape[2]
    head_width = width // HEADS
    up_rows = upstream[0]

    def split_heads(array):
        return array.reshape(local_rows, HEADS, head_width)

    query_heads = split_heads(queries[0])
    key_heads = split_heads(keys[0])
    value_heads = split_heads(values[0])
    grad_att = project_back(up_rows, w_out)
    head_q, head_k, head_v, head_g = (
        lax.all_to_all(query_heads, "seq", split_axis=1, concat_axis=0, tiled=True),
        lax.all_to_all(key_heads, "seq", split_axis=1, concat_axis=0, tiled=True),
        lax.all_to_all(value_heads, "seq", split_axis=1, concat_axis=0, tiled=True),
        lax.all_to_all(split_heads(grad_att), "seq", split_axis=1, concat_axis=0, tiled=True),
    )
    attended, grad_query, grad_key, grad_value = block_attention(
        head_q, head_k, head_v, head_g, key_blocks[0], block_counts[0]
    )
    node_att, node_gq, node_gk, node_gv = (
        lax.all_to_all(attended, "seq", split_axis=0, concat_axis=1, tiled=True),
        lax.all_to_all(grad_query, "seq", split_axis=0, concat_axis=1, tiled=True),
        lax.all_to_all(grad_key, "seq", split_axis=0, concat_axis=1, tiled=True),
        lax.all_to_all(grad_value, "seq", split_axis=0, concat_axis=1, tiled=True),
    )
    att_nodes = node_att.reshape(local_rows, width)
    mixed = jnp.dot(att_nodes, w_out, preferred_element_type=jnp.float32).astype(jnp.bfloat16)
    factor = 1.0 / math.sqrt(lax.axis_size("dp") * lax.axis_size("seq") * local_rows)
    summed = lax.psum_scatter(
        inner_rows(att_nodes, up_rows), "seq", scatter_dimension=0, tiled=True
    )
    grad_wo = lax.psum_scatter(summed, "dp", scatter_dimension=1, tiled=True)
    full_shape = (1, local_rows, width)
    return (
        mixed.reshape(full_shape),
        node_gq.reshape(full_shape),
        node_gk.reshape(full_shape),
        node_gv.reshape(full_shape),
        grad_wo * factor,
    )


MESH = pl.DeviceIdType.MESH
LANES = 128
MASKED = -1e30


def dot_nt(left, right):
    return lax.dot_general(
        left, right, (((1,), (1,)), ((), ())), preferred_element_type=jnp.float32
    )


def fused(
    peers, levels, head_width, factor, list_ref, count_ref, q_hbm, k_hbm, v_hbm, u_hbm, w_hbm,
    mixed_hbm, gq_hbm, gk_hbm, gv_hbm, gw_ref,
    head_q, head_g, keys2, values2, g_local, out_stage, key_sum, value_sum, att_nodes,
    kept_weights, kept_inverse, kept_logits,
    q_ref, k_ref, v_ref, u_ref, w_ref, mixed_ref, gq_ref, gk_ref, gv_ref,
    gw_other, gw_own, gw_core, gw_level, gw_levels, gw_seq, gw_seqs,
    send_in, recv_in, send_out, recv_out, own_sem,
    send_core, recv_core, send_level, recv_level, send_seq, recv_seq,
    load_sem, own_out, mixed_sem,
):
    me = lax.axis_index("seq")
    replica = lax.axis_index("dp")
    core = lax.rem(replica, 2)
    level = replica // 2
    rows = q_ref.shape[0]
    chunks = head_q.shape[0]
    nodes = head_q.shape[1]
    listed, blocks = list_ref.shape
    block_rows = nodes // blocks
    per_device = blocks // peers
    span = chunks * LANES
    score_scale = 1.0 / math.sqrt(head_width)
    bf16, f32 = jnp.bfloat16, jnp.float32

    loads = [
        pltpu.make_async_copy(there, here, load_sem.at[at])
        for at, (there, here) in enumerate(
            [(q_hbm, q_ref), (k_hbm, k_ref), (v_hbm, v_ref), (u_hbm, u_ref), (w_hbm, w_ref)]
        )
    ]
    for load in loads:
        load.start()
    barrier = pltpu.get_barrier_semaphore()
    for p in range(1, peers):
        pl.semaphore_signal(
            barrier, inc=1, device_id={"seq": lax.rem(me + p, peers)}, device_id_type=MESH
        )
    other_core = level * 2 + 1 - core

    def level_at(p):
        return lax.rem(level + p, levels)

    pl.semaphore_signal(barrier, inc=1, device_id={"dp": other_core}, device_id_type=MESH)
    for p in range(1, levels):
        pl.semaphore_signal(
            barrier, inc=1, device_id={"dp": level_at(p) * 2 + core}, device_id_type=MESH
        )
    pl.semaphore_wait(barrier, peers + levels - 1)

    own_rows = pl.ds(pl.multiple_of(me * rows, rows), rows)

    def columns(device, c):
        return pl.ds(pl.multiple_of(device * span + c * LANES, LANES), LANES)

    sources = (q_ref, k_ref, v_ref, g_local)
    targets = (head_q, keys2, values2, head_g)

    def landing(a, c):
        if a in (1, 2):
            return targets[a][c].at[pl.ds(me * per_device, per_device), :, pl.ds(0, LANES)]
        return targets[a].at[c, own_rows]

    def leaving(a, device, c):
        if a in (1, 2):
            return sources[a].at[:, :, columns(device, c)]
        return sources[a].at[:, columns(device, c)]

    def inward(a, c, p):
        device = lax.rem(me + p, peers)
        return pltpu.make_async_remote_copy(
            src_ref=leaving(a, device, c),
            dst_ref=landing(a, c),
            send_sem=send_in.at[c, a, p - 1],
            recv_sem=recv_in.at[c, a, p - 1],
            device_id={"seq": device},
            device_id_type=MESH,
        )

    def own_copy(a, c):
        return pltpu.make_async_copy(
            leaving(a, me, c), landing(a, c), own_sem.at[c, a]
        )

    def start_in(a, c):
        for p in range(1, peers):
            inward(a, c, p).start()
        own_copy(a, c).start()

    def finish_in(a, c):
        for p in range(1, peers):
            inward(a, c, p).wait()
        own_copy(a, c).wait()

    returns = (att_nodes, gq_ref, gk_ref, gv_ref)

    def outward(a, c, p):
        device = lax.rem(me + p, peers)
        return pltpu.make_async_remote_copy(
            src_ref=out_stage.at[c, a, pl.ds(pl.multiple_of(device * rows, rows), rows)],
            dst_ref=returns[a].at[:, columns(me, c)],
            send_sem=send_out.at[c, a, p - 1],
            recv_sem=recv_out.at[c, a, p - 1],
            device_id={"seq": device},
            device_id_type=MESH,
        )

    def keep_own(a, c):
        return pltpu.make_async_copy(
            out_stage.at[c, a, own_rows], returns[a].at[:, columns(me, c)], own_out.at[c, a]
        )

    def grad_att(c):
        def one(device, carry):
            cols = columns(device, c)
            g_local[:, cols] = dot_nt(u_ref[...], w_ref[cols, :]).astype(bf16)
            return carry

        lax.fori_loop(0, peers, one, 0)

    lane = lax.broadcasted_iota(jnp.int32, (block_rows, LANES), 1)
    lane2 = lax.broadcasted_iota(jnp.int32, (2 * block_rows, LANES), 1)
    first = lane < head_width

    def stacked(x):
        return jnp.concatenate([jnp.where(first, x, 0.0), jnp.where(first, 0.0, x)], axis=0)

    def merged(x):
        return jnp.where(first, x[:block_rows], x[block_rows:])

    def core_copy(c):
        return pltpu.make_async_remote_copy(
            src_ref=gw_other.at[c], dst_ref=gw_core.at[c],
            send_sem=send_core.at[c], recv_sem=recv_core.at[c],
            device_id={"dp": other_core}, device_id_type=MESH,
        )

    def level_copy(c, p):
        return pltpu.make_async_remote_copy(
            src_ref=gw_level.at[c, level_at(p)], dst_ref=gw_levels.at[c, p - 1],
            send_sem=send_level.at[c, p - 1], recv_sem=recv_level.at[c, p - 1],
            device_id={"dp": level_at(p) * 2 + core}, device_id_type=MESH,
        )

    def seq_copy(c, p):
        device = lax.rem(me + p, peers)
        return pltpu.make_async_remote_copy(
            src_ref=gw_seq.at[c, pl.ds(pl.multiple_of(device * LANES, LANES), LANES)],
            dst_ref=gw_seqs.at[c, p - 1],
            send_sem=send_seq.at[c, p - 1], recv_sem=recv_seq.at[c, p - 1],
            device_id={"seq": device}, device_id_type=MESH,
        )

    def gw_partial(c):
        for p in range(1, peers):
            outward(0, c, p).wait()
        keep_own(0, c).wait()

        def up_columns(which):
            return jnp.concatenate(
                [
                    u_ref[:, pl.ds(pl.multiple_of((at * 2 + which) * LANES, LANES), LANES)]
                    for at in range(levels)
                ],
                axis=1,
            )

        def one(device, carry):
            place = pl.ds(pl.multiple_of(device * LANES, LANES), LANES)
            att = att_nodes[:, columns(device, c)]
            theirs = inner_rows(att, up_columns(1 - core)).astype(bf16)
            ours = inner_rows(att, up_columns(core))
            for at in range(levels):
                cut = slice(at * LANES, (at + 1) * LANES)
                gw_other[c, at, place, :] = theirs[:, cut]
                gw_own[c, at, place, :] = ours[:, cut]
            return carry

        lax.fori_loop(0, peers, one, 0)
        core_copy(c).start()

    def gw_across_levels(c):
        core_copy(c).wait()

        def one(at, carry):
            total = gw_own[c, at] + gw_core[c, at].astype(f32)
            gw_own[c, at] = total
            gw_level[c, at] = total.astype(bf16)
            return carry

        lax.fori_loop(0, levels, one, 0)
        for p in range(1, levels):
            level_copy(c, p).start()

    def gw_across_seq(c):
        total = gw_own[c, level]
        for p in range(1, levels):
            level_copy(c, p).wait()
            total = total + gw_levels[c, p - 1].astype(f32)
        gw_own[c, level] = total
        gw_seq[c] = total.astype(bf16)
        for p in range(1, peers):
            seq_copy(c, p).start()

    def gw_finish(c):
        total = gw_own[c, level, pl.ds(pl.multiple_of(me * LANES, LANES), LANES), :]
        for p in range(1, peers):
            seq_copy(c, p).wait()
            total = total + gw_seqs[c, p - 1].astype(f32)
        gw_ref[c * LANES:(c + 1) * LANES, :] = total * factor

    def dest_blocks(p):
        device = lax.rem(me + p, peers)
        return [device * per_device + at for at in range(per_device)]

    def rows_of(b):
        return pl.ds(pl.multiple_of(b * block_rows, block_rows), block_rows)

    def listed_rows(table, b):
        return jnp.concatenate([table[list_ref[j, b]] for j in range(listed)], axis=0)

    def run_between(p, between):
        for at, step in between:
            pl.when(p == at)(step)

    def forward(c):
        def one_group(step, carry):
            p = step + 1
            group = dest_blocks(p)
            lefts = []
            for b in group:
                q = head_q[c, rows_of(b), :].astype(f32) * score_scale
                count = count_ref[b]
                used = lane2 < 0
                for j in range(listed):
                    used = used | (lane2 == jnp.where(j < count, list_ref[j, b], -1))
                bias = jnp.where(used, 0.0, MASKED)
                lefts.append(jnp.concatenate([stacked(q), bias], axis=1).astype(bf16))
            scores = [dot_nt(left, listed_rows(keys2[c], b)) for left, b in zip(lefts, group)]
            tops = [jnp.max(score, axis=1, keepdims=True) for score in scores]
            weights = [jnp.exp(score - top).astype(bf16) for score, top in zip(scores, tops)]
            sums = [
                jnp.dot(weight, listed_rows(values2[c], b), preferred_element_type=f32)
                for weight, b in zip(weights, group)
            ]
            for b, weight, summed in zip(group, weights, sums):
                for j in range(listed):
                    kept_weights[c, b, j] = weight[:, j * block_rows:(j + 1) * block_rows]
                inverse = 1.0 / summed[:, LANES:LANES + 1]
                kept_inverse[c, b] = jnp.broadcast_to(inverse, (2 * block_rows, LANES))
                out_stage[c, 0, rows_of(b), :] = merged(summed[:, :LANES] * inverse).astype(bf16)

            @pl.when(p < peers)
            def _():
                outward(0, c, p).start()

            return carry

        lax.fori_loop(0, peers, one_group, 0)
        keep_own(0, c).start()

    def backward(c, between):
        key_sum[...] = jnp.zeros_like(key_sum)
        value_sum[...] = jnp.zeros_like(value_sum)

        def one_group(step, carry):
            p = step + 1
            group = dest_blocks(p)
            q_sides, g_sides, rights = [], [], []
            for b in group:
                inverse = kept_inverse[c, b]
                q_pair = stacked(head_q[c, rows_of(b), :].astype(f32) * score_scale)
                g_pair = stacked(head_g[c, rows_of(b), :].astype(f32))
                attended = out_stage[c, 0, rows_of(b), :].astype(f32)
                delta = jnp.sum(
                    g_pair * jnp.concatenate([attended, attended], axis=0), axis=1, keepdims=True
                )
                high = delta.astype(bf16).astype(f32)
                middle = (delta - high).astype(bf16).astype(f32)
                low = delta - high - middle
                shift = jnp.where(
                    lane2 == 0, -high,
                    jnp.where(lane2 == 1, -middle, jnp.where(lane2 == 2, -low, 0.0)),
                )
                q_sides.append((q_pair * inverse).astype(bf16))
                g_sides.append((g_pair * inverse).astype(bf16))
                rights.append(jnp.concatenate([g_pair, shift], axis=1).astype(bf16))
            shifted = [dot_nt(right, listed_rows(values2[c], b)) for right, b in zip(rights, group)]
            for at, b in enumerate(group):
                for j in range(listed):
                    cut = slice(j * block_rows, (j + 1) * block_rows)
                    kept_logits[at, j] = (
                        kept_weights[c, b, j].astype(f32) * shifted[at][:, cut]
                    ).astype(bf16)
            wide_logits, wide_weights = [], []
            for at, b in enumerate(group):
                logits = jnp.concatenate([kept_logits[at, j] for j in range(listed)], axis=1)
                grad_q = jnp.dot(
                    logits, listed_rows(keys2[c], b)[:, :LANES],
                    preferred_element_type=f32,
                )
                grad_q = merged(grad_q * (kept_inverse[c, b] * score_scale))
                out_stage[c, 1, rows_of(b), :] = grad_q.astype(bf16)
                slots = []
                for key_block in range(blocks):
                    slot = jnp.int32(listed)
                    for j in range(listed):
                        slot = jnp.where(list_ref[j, b] == key_block, j, slot)
                    slots.append(slot)
                wide_logits.append(jnp.concatenate([kept_logits[at, i] for i in slots], axis=1))
                wide_weights.append(jnp.concatenate([kept_weights[c, b, i] for i in slots], axis=1))
            key_sum[...] += inner_rows(
                jnp.concatenate(q_sides, axis=0), jnp.concatenate(wide_logits, axis=0)
            )
            value_sum[...] += inner_rows(
                jnp.concatenate(g_sides, axis=0), jnp.concatenate(wide_weights, axis=0)
            )

            @pl.when(p < peers)
            def _():
                outward(1, c, p).start()

            run_between(p, between)
            return carry

        lax.fori_loop(0, peers, one_group, 0)
        out_stage[c, 2] = key_sum[...].T.astype(bf16)
        for p in range(1, peers):
            outward(2, c, p).start()
        out_stage[c, 3] = value_sum[...].T.astype(bf16)
        for p in range(1, peers):
            outward(3, c, p).start()
        for a in range(1, 4):
            keep_own(a, c).start()

    def project():
        mixed_ref[...] = jnp.dot(
            att_nodes[...], w_ref[...], preferred_element_type=f32
        ).astype(bf16)

    for a in range(3):
        loads[a].wait()
        start_in(a, 0)
    loads[3].wait()
    loads[4].wait()
    grad_att(0)
    start_in(3, 0)
    for c in range(1, chunks):
        grad_att(c)
    block_of = lax.broadcasted_iota(jnp.int32, (blocks, block_rows, LANES), 0)
    node_lane = lax.broadcasted_iota(jnp.int32, (blocks, block_rows, LANES), 2)
    for c in range(chunks):
        keys2[c][:, :, LANES:] = jnp.where(node_lane == block_of, 1.0, 0.0).astype(bf16)
        values2[c][:, :, LANES:] = jnp.where(node_lane < 3, 1.0, 0.0).astype(bf16)
    nothing = jnp.zeros((2 * block_rows, block_rows), bf16)
    for c in range(chunks):
        for b in range(blocks):
            kept_weights[c, b, listed] = nothing
    for at in range(per_device):
        kept_logits[at, listed] = nothing
    last = chunks - 1
    for c in range(chunks):
        for a in range(3):
            finish_in(a, c)
            if a == 1 and c < last:
                for later in range(4):
                    start_in(later, c + 1)
        forward(c)
        finish_in(3, c)
        between = [
            (2, functools.partial(gw_partial, c)),
            (3, functools.partial(gw_across_levels, c)),
        ]
        if c > 0:
            between.append((1, functools.partial(gw_across_seq, c - 1)))
        if c == last:
            between.append((4, project))
        backward(c, between)
    stores = [
        pltpu.make_async_copy(here, there, mixed_sem.at[a])
        for a, (here, there) in enumerate(
            [(mixed_ref, mixed_hbm), (gq_ref, gq_hbm), (gk_ref, gk_hbm), (gv_ref, gv_hbm)]
        )
    ]
    stores[0].start()
    for a in range(1, 4):
        for c in range(chunks):
            for p in range(1, peers):
                outward(a, c, p).wait()
            keep_own(a, c).wait()
        if a == 1:
            gw_across_seq(last)
        stores[a].start()
    for c in range(chunks):
        gw_finish(c)
    for store in stores:
        store.wait()


def copy_out(count, *refs):
    sources, targets, held = refs[:count], refs[count:2 * count], refs[2 * count]
    loaded, stored = refs[2 * count + 1:]
    loads = [pltpu.make_async_copy(sources[i], held[i], loaded.at[i]) for i in range(count)]
    stores = [pltpu.make_async_copy(held[i], targets[i], stored.at[i]) for i in range(count)]
    for load in loads:
        load.start()
    for load, store in zip(loads, stores):
        load.wait()
        store.start()
    for store in stores:
        store.wait()


def local_fused(queries, keys, values, upstream, w_out, key_blocks, block_counts):
    rows, width = queries.shape[1:]
    peers = lax.axis_size("seq")
    chunks = width // peers // LANES
    nodes = rows * peers
    bf16, f32 = jnp.bfloat16, jnp.float32
    replicas = lax.axis_size("dp")
    levels = replicas // 2
    blocks, listed = key_blocks.shape[1:]
    block_rows = nodes // blocks
    by_block = (blocks // peers, block_rows, width)
    factor = 1.0 / math.sqrt(replicas * nodes)
    vmem = pl.BlockSpec(memory_space=pltpu.VMEM)
    anywhere = pl.BlockSpec(memory_space=pl.ANY)
    smem = pl.BlockSpec(memory_space=pltpu.SMEM)
    part = jax.ShapeDtypeStruct((rows, width), bf16)
    results = pl.pallas_call(
        functools.partial(fused, peers, levels, width // HEADS, factor),
        out_shape=(part, part, part, part, jax.ShapeDtypeStruct((chunks * LANES, width // replicas), f32)),
        in_specs=[smem, smem] + [anywhere] * 5,
        out_specs=[anywhere] * 4 + [vmem],
        scratch_shapes=[
            pltpu.VMEM((chunks, nodes, LANES), bf16),
            pltpu.VMEM((chunks, nodes, LANES), bf16),
            tuple(pltpu.VMEM((blocks, block_rows, 2 * LANES), bf16) for _ in range(chunks)),
            tuple(pltpu.VMEM((blocks, block_rows, 2 * LANES), bf16) for _ in range(chunks)),
            pltpu.VMEM((rows, width), bf16),
            pltpu.VMEM((chunks, 4, nodes, LANES), bf16),
            pltpu.VMEM((LANES, nodes), f32),
            pltpu.VMEM((LANES, nodes), f32),
            pltpu.VMEM((rows, width), bf16),
            pltpu.VMEM((chunks, blocks, listed + 1, 2 * block_rows, block_rows), bf16),
            pltpu.VMEM((chunks, blocks, 2 * block_rows, LANES), f32),
            pltpu.VMEM((blocks // peers, listed + 1, 2 * block_rows, block_rows), bf16),
            pltpu.VMEM((rows, width), bf16),
            pltpu.VMEM(by_block, bf16),
            pltpu.VMEM(by_block, bf16),
            pltpu.VMEM((rows, width), bf16),
            pltpu.VMEM((width, width), bf16),
            pltpu.VMEM((rows, width), bf16),
            pltpu.VMEM((rows, width), bf16),
            pltpu.VMEM((rows, width), bf16),
            pltpu.VMEM((rows, width), bf16),
            pltpu.VMEM((chunks, levels, peers * LANES, LANES), bf16),
            pltpu.VMEM((chunks, levels, peers * LANES, LANES), f32),
            pltpu.VMEM((chunks, levels, peers * LANES, LANES), bf16),
            pltpu.VMEM((chunks, levels, peers * LANES, LANES), bf16),
            pltpu.VMEM((chunks, levels - 1, peers * LANES, LANES), bf16),
            pltpu.VMEM((chunks, peers * LANES, LANES), bf16),
            pltpu.VMEM((chunks, peers - 1, LANES, LANES), bf16),
            pltpu.SemaphoreType.DMA((chunks, 4, peers - 1)),
            pltpu.SemaphoreType.DMA((chunks, 4, peers - 1)),
            pltpu.SemaphoreType.DMA((chunks, 4, peers - 1)),
            pltpu.SemaphoreType.DMA((chunks, 4, peers - 1)),
            pltpu.SemaphoreType.DMA((chunks, 4)),
            pltpu.SemaphoreType.DMA((chunks,)),
            pltpu.SemaphoreType.DMA((chunks,)),
            pltpu.SemaphoreType.DMA((chunks, levels - 1)),
            pltpu.SemaphoreType.DMA((chunks, levels - 1)),
            pltpu.SemaphoreType.DMA((chunks, peers - 1)),
            pltpu.SemaphoreType.DMA((chunks, peers - 1)),
            pltpu.SemaphoreType.DMA((5,)),
            pltpu.SemaphoreType.DMA((chunks, 4)),
            pltpu.SemaphoreType.DMA((4,)),
        ],
        compiler_params=pltpu.CompilerParams(
            collective_id=0, has_side_effects=True, vmem_limit_bytes=56 * 1024 * 1024
        ),
        name="graph_attention",
    )(
        key_blocks[0].T, block_counts[0], queries[0], keys.reshape(by_block),
        values.reshape(by_block), upstream[0], w_out,
    )
    count = len(results)
    mixed, grad_q, grad_k, grad_v, grad_wo = pl.pallas_call(
        functools.partial(copy_out, count),
        out_shape=[jax.ShapeDtypeStruct(result.shape, result.dtype) for result in results],
        in_specs=[anywhere] * count,
        out_specs=[anywhere] * count,
        scratch_shapes=[
            tuple(pltpu.VMEM(result.shape, result.dtype) for result in results),
            pltpu.SemaphoreType.DMA((count,)),
            pltpu.SemaphoreType.DMA((count,)),
        ],
        compiler_params=pltpu.CompilerParams(vmem_limit_bytes=56 * 1024 * 1024),
        name="copy_out",
    )(*results)
    return mixed[None], grad_q[None], grad_k[None], grad_v[None], grad_wo


def local(queries, keys, values, upstream, w_out, key_blocks, block_counts):
    width = queries.shape[2]
    peers = lax.axis_size("seq")
    pair = 2 * (width // HEADS) == LANES and width % (peers * LANES) == 0
    whole_blocks = key_blocks.shape[1] % peers == 0 and key_blocks.shape[1] <= LANES
    whole_blocks = whole_blocks and peers >= 4
    columns_fit = lax.axis_size("dp") * LANES == width
    chosen = local_fused if pair and whole_blocks and columns_fit else local_plain
    return chosen(queries, keys, values, upstream, w_out, key_blocks, block_counts)


def solution(mesh):
    placed = (
        P("dp", "seq", None),
        P("dp", "seq", None),
        P("dp", "seq", None),
        P("dp", "seq", None),
        P(),
        P("dp", None, None),
        P("dp", None),
    )
    return jax.shard_map(
        local,
        mesh=mesh,
        in_specs=placed,
        out_specs=(
            P("dp", "seq", None),
            P("dp", "seq", None),
            P("dp", "seq", None),
            P("dp", "seq", None),
            P("seq", "dp"),
        ),
        check_vma=False,
    )
```

profile of v0, /device:TPU:0, one launch (start us, length us, event | category | flops | bytes accessed | tf_op | source)
XLA Modules:
  0.0 72.9 jit_solution(15580029720249770155)
XLA Ops:
  0.6 69.8 %graph_attention.1 = (bf16[256,1024]{1,0:T(8,128)(2,1)}, bf16[256,1024]{1,0:T(8,128)(2,1)}, bf16[256,1024]{1,0:T(8,128)(2,1)}, bf16[256,1024]{1,0:T(8,128)(2,1)}, f32[256,128]{1,0:T(8,128)}) custom-call(s32[4,8]{1,0:T(4,128)} %bitcast.16, s32[8]{0:T(128)} %bitcast.17, bf16[256,1024]{1,0:T(8,128)(2,1)} %bitcast.12, bf16[2,128,1024]{2,1,0:T(8,128)(2,1)} %bitcast.13, ...), custom_call_target="tpu_custom_call" | custom-call | tf_op jit(solution)/shard_map/graph_attention/pallas_call | solution.py:576
  70.4 2.5 %copy_out.1 = (bf16[256,1024]{1,0:T(8,128)(2,1)}, bf16[256,1024]{1,0:T(8,128)(2,1)}, bf16[256,1024]{1,0:T(8,128)(2,1)}, bf16[256,1024]{1,0:T(8,128)(2,1)}, f32[256,128]{1,0:T(8,128)}) custom-call(bf16[256,1024]{1,0:T(8,128)(2,1)} %get-tuple-element.15.refs_0_, bf16[256,1024]{1,0:T(8,128)(2,1)} %get-tuple-element.16.refs_1_, ...), custom_call_target="tpu_custom_call" | custom-call | tf_op jit(solution)/shard_map/copy_out/pallas_call | solution.py:634
where the time goes:
time: 74.1 us; the launch traced here: 72.9 us
  Pallas kernels  72.3 us (98%)
    pallas_call x1, Pallas kernels, local_fused(): pl.pallas_call(functools.partial(fused, peers, levels, width // HEADS, fa...  69.8 us
    pallas_call x1, Pallas kernels, local_fused(): pl.pallas_call(functools.partial(copy_out, count), out_shape=[jax.ShapeDt...  2.47 us

commit v1 on v0

--- a/solution.py
+++ b/solution.py
@@ -150,7 +150,7 @@
     head_q, head_g, keys2, values2, g_local, out_stage, key_sum, value_sum, att_nodes,
     kept_weights, kept_inverse, kept_logits,
     q_ref, k_ref, v_ref, u_ref, w_ref, mixed_ref, gq_ref, gk_ref, gv_ref,
-    gw_other, gw_own, gw_core, gw_level, gw_levels, gw_seq, gw_seqs,
+    gw_other, gw_own, gw_core, gw_seq, gw_seqs, gw_half, gw_level, gw_levels,
     send_in, recv_in, send_out, recv_out, own_sem,
     send_core, recv_core, send_level, recv_level, send_seq, recv_seq,
     load_sem, own_out, mixed_sem,
@@ -291,7 +291,7 @@
     def seq_copy(c, p):
         device = lax.rem(me + p, peers)
         return pltpu.make_async_remote_copy(
-            src_ref=gw_seq.at[c, pl.ds(pl.multiple_of(device * LANES, LANES), LANES)],
+            src_ref=gw_seq.at[c, :, pl.ds(pl.multiple_of(device * LANES, LANES), LANES)],
             dst_ref=gw_seqs.at[c, p - 1],
             send_sem=send_seq.at[c, p - 1], recv_sem=recv_seq.at[c, p - 1],
             device_id={"seq": device}, device_id_type=MESH,
@@ -325,34 +325,36 @@
         lax.fori_loop(0, peers, one, 0)
         core_copy(c).start()
 
-    def gw_across_levels(c):
+    own_part = pl.ds(pl.multiple_of(me * LANES, LANES), LANES)
+
+    def gw_across_seq(c):
         core_copy(c).wait()
 
         def one(at, carry):
             total = gw_own[c, at] + gw_core[c, at].astype(f32)
             gw_own[c, at] = total
-            gw_level[c, at] = total.astype(bf16)
+            gw_seq[c, at] = total.astype(bf16)
             return carry
 
         lax.fori_loop(0, levels, one, 0)
+        for p in range(1, peers):
+            seq_copy(c, p).start()
+
+    def gw_across_levels(c):
+        total = gw_own[c, :, own_part, :]
+        for p in range(1, peers):
+            seq_copy(c, p).wait()
+            total = total + gw_seqs[c, p - 1].astype(f32)
+        gw_half[c] = total
+        gw_level[c] = total.astype(bf16)
         for p in range(1, levels):
             level_copy(c, p).start()
 
-    def gw_across_seq(c):
-        total = gw_own[c, level]
+    def gw_finish(c):
+        total = gw_half[c, level]
         for p in range(1, levels):
             level_copy(c, p).wait()
             total = total + gw_levels[c, p - 1].astype(f32)
-        gw_own[c, level] = total
-        gw_seq[c] = total.astype(bf16)
-        for p in range(1, peers):
-            seq_copy(c, p).start()
-
-    def gw_finish(c):
-        total = gw_own[c, level, pl.ds(pl.multiple_of(me * LANES, LANES), LANES), :]
-        for p in range(1, peers):
-            seq_copy(c, p).wait()
-            total = total + gw_seqs[c, p - 1].astype(f32)
         gw_ref[c * LANES:(c + 1) * LANES, :] = total * factor
 
     def dest_blocks(p):
@@ -369,7 +371,7 @@
         for at, step in between:
             pl.when(p == at)(step)
 
-    def forward(c):
+    def forward(c, between):
         def one_group(step, carry):
             p = step + 1
             group = dest_blocks(p)
@@ -400,6 +402,7 @@
             def _():
                 outward(0, c, p).start()
 
+            run_between(p, between)
             return carry
 
         lax.fori_loop(0, peers, one_group, 0)
@@ -489,9 +492,7 @@
         start_in(a, 0)
     loads[3].wait()
     loads[4].wait()
-    grad_att(0)
-    start_in(3, 0)
-    for c in range(1, chunks):
+    for c in range(chunks):
         grad_att(c)
     block_of = lax.broadcasted_iota(jnp.int32, (blocks, block_rows, LANES), 0)
     node_lane = lax.broadcasted_iota(jnp.int32, (blocks, block_rows, LANES), 2)
@@ -509,17 +510,26 @@
         for a in range(3):
             finish_in(a, c)
             if a == 1 and c < last:
-                for later in range(4):
+                for later in range(3):
                     start_in(later, c + 1)
-        forward(c)
+            if a == 1 and c == last:
+                for every in range(chunks):
+                    start_in(3, every)
+        between = []
+        if c > 0:
+            between.append((2, functools.partial(gw_partial, c - 1)))
+            between.append((4, functools.partial(gw_across_seq, c - 1)))
+        forward(c, between)
+    for c in range(chunks):
         finish_in(3, c)
-        between = [
-            (2, functools.partial(gw_partial, c)),
-            (3, functools.partial(gw_across_levels, c)),
-        ]
-        if c > 0:
-            between.append((1, functools.partial(gw_across_seq, c - 1)))
+        between = []
         if c == last:
+            between.append((1, functools.partial(gw_across_levels, last)))
+        if c == 0:
+            for early in range(last):
+                between.append((1, functools.partial(gw_across_levels, early)))
+            between.append((2, functools.partial(gw_partial, last)))
+            between.append((3, functools.partial(gw_across_seq, last)))
             between.append((4, project))
         backward(c, between)
     stores = [
@@ -534,8 +544,6 @@
             for p in range(1, peers):
                 outward(a, c, p).wait()
             keep_own(a, c).wait()
-        if a == 1:
-            gw_across_seq(last)
         stores[a].start()
     for c in range(chunks):
         gw_finish(c)
@@ -604,9 +612,10 @@
             pltpu.VMEM((chunks, levels, peers * LANES, LANES), f32),
             pltpu.VMEM((chunks, levels, peers * LANES, LANES), bf16),
             pltpu.VMEM((chunks, levels, peers * LANES, LANES), bf16),
-            pltpu.VMEM((chunks, levels - 1, peers * LANES, LANES), bf16),
-            pltpu.VMEM((chunks, peers * LANES, LANES), bf16),
-            pltpu.VMEM((chunks, peers - 1, LANES, LANES), bf16),
+            pltpu.VMEM((chunks, peers - 1, levels, LANES, LANES), bf16),
+            pltpu.VMEM((chunks, levels, LANES, LANES), f32),
+            pltpu.VMEM((chunks, levels, LANES, LANES), bf16),
+            pltpu.VMEM((chunks, levels - 1, LANES, LANES), bf16),
             pltpu.SemaphoreType.DMA((chunks, 4, peers - 1)),
             pltpu.SemaphoreType.DMA((chunks, 4, peers - 1)),
             pltpu.SemaphoreType.DMA((chunks, 4, peers - 1)),

time: 74.1 us -> 75.1 us (1.013); the launches traced: 72.9 us -> 74.9 us
  Pallas kernels: 72.3 us -> 74.3 us
    pallas_call x1, Pallas kernels: 69.8 us -> 71.8 us  [local_fused(): pl.pallas_call(functools.partial(fused, peers, levels, width // HEADS, fa...]
where the time goes in v1:
time: 75.1 us; the launch traced here: 74.9 us
  Pallas kernels  74.3 us (99%)
    pallas_call x1, Pallas kernels, local_fused(): pl.pallas_call(functools.partial(fused, peers, levels, width // HEADS, fa...  71.8 us
    pallas_call x1, Pallas kernels, local_fused(): pl.pallas_call(functools.partial(copy_out, count), out_shape=[jax.ShapeDt...  2.47 us

profile of v1, /device:TPU:0, one launch (start us, length us, event | category | flops | bytes accessed | tf_op | source)
XLA Modules:
  0.0 74.9 jit_solution(12238831943327063353)
XLA Ops:
  0.6 71.8 %graph_attention.1 = (bf16[256,1024]{1,0:T(8,128)(2,1)}, bf16[256,1024]{1,0:T(8,128)(2,1)}, bf16[256,1024]{1,0:T(8,128)(2,1)}, bf16[256,1024]{1,0:T(8,128)(2,1)}, f32[256,128]{1,0:T(8,128)}) custom-call(s32[4,8]{1,0:T(4,128)} %bitcast.16, s32[8]{0:T(128)} %bitcast.17, bf16[256,1024]{1,0:T(8,128)(2,1)} %bitcast.12, bf16[2,128,1024]{2,1,0:T(8,128)(2,1)} %bitcast.13, ...), custom_call_target="tpu_custom_call" | custom-call | tf_op jit(solution)/shard_map/graph_attention/pallas_call | solution.py:584
  72.5 2.5 %copy_out.1 = (bf16[256,1024]{1,0:T(8,128)(2,1)}, bf16[256,1024]{1,0:T(8,128)(2,1)}, bf16[256,1024]{1,0:T(8,128)(2,1)}, bf16[256,1024]{1,0:T(8,128)(2,1)}, f32[256,128]{1,0:T(8,128)}) custom-call(bf16[256,1024]{1,0:T(8,128)(2,1)} %get-tuple-element.15.refs_0_, bf16[256,1024]{1,0:T(8,128)(2,1)} %get-tuple-element.16.refs_1_, ...), custom_call_target="tpu_custom_call" | custom-call | tf_op jit(solution)/shard_map/copy_out/pallas_call | solution.py:643
